TPU v7x, 32 devices: a whole 2x2x4 slice. The times are simulated.
32 devices in a mesh: seq: 2 (over core), heads: 4 (over y, x), dp: 4 (over z).
Axes of the slice: x: 2, y: 2, z: 4, core: 2. Of those that a mesh axis runs over, the one named last changes fastest.
Arguments:
- tokens: bfloat16 [4, 256, 3072], P('dp', 'seq'), may hold values from -6 to 6
- proj_weights: bfloat16 [3, 3072, 4096], P(None, 'seq', ('heads', 'dp')), may hold values from -0.109375 to 0.109375
- norm_gain: float32 [4096], P(('heads', 'dp')), may hold values from 0.5 to 1.5
Outputs:
- attended: bfloat16 [4, 256, 4096], P('dp', 'seq', 'heads')
All inputs are finite; a program needn't handle non-finite values.
Results may differ from a plain program's by a relative error of at most 0.0063.
Values may be sent and summed in bfloat16 or wider, within the bound.
A program may use at most 64 MiB of HBM per device.

v0:
```python
import jax
import jax.numpy as jnp
from jax import lax
from jax.sharding import PartitionSpec as P

DH = 128


def prefix_2(part, axis, combine, identity):
    place = lax.axis_index(axis)
    gathered = lax.all_gather(part, axis)
    state = jnp.zeros_like(part) + jnp.asarray(identity, part.dtype)

    def one(step, state):
        return combine(state, lax.dynamic_index_in_dim(gathered, step, 0, False))

    return lax.fori_loop(0, place, one, state)


def add_pair(earlier, later):
    return earlier + later


def project_rows(flat_rows):

    def accumulate(total, piece, start):
        return jnp.einsum("nd,jdc->jnc", flat_rows, piece, preferred_element_type=jnp.float32)

    return accumulate


def to_heads(matrix, seq_count, length):
    return matrix.reshape(seq_count, length, -1, DH)


def activate(matrix, seq_count, length):
    return to_heads(jax.nn.silu(matrix).astype(jnp.bfloat16), seq_count, length)


def block_prefix(keys_b, values_b):
    state = jnp.einsum("sthd,sthe->shde", keys_b, values_b, preferred_element_type=jnp.float32)
    return prefix_2(state, "seq", add_pair, jnp.zeros_like(state))


def attend(queries, keys_b, values_b, prefix, norm_gain):
    seq_count, length, head_count, head_size = queries.shape
    scores = jnp.einsum("sthd,suhd->shtu", queries, keys_b, preferred_element_type=jnp.float32)
    causal = lax.broadcasted_iota(jnp.int32, (length, length), 0) >= lax.broadcasted_iota(
        jnp.int32, (length, length), 1
    )
    scores_b = jnp.where(causal, scores, 0.0).astype(jnp.bfloat16)
    local = jnp.einsum("shtu,suhd->sthd", scores_b, values_b, preferred_element_type=jnp.float32)
    carried = jnp.einsum(
        "sthd,shde->sthe", queries, prefix.astype(jnp.bfloat16), preferred_element_type=jnp.float32
    )
    attn = local + carried
    scale = lax.rsqrt(jnp.mean(attn * attn, axis=-1, keepdims=True) + 1e-06)
    normed = attn * scale * norm_gain.reshape(head_count, head_size)
    return normed.astype(jnp.bfloat16).reshape(seq_count, length, head_count * head_size)


def body(tokens, proj_weights, norm_gain):
    everyone = lax.all_gather(tokens, "dp", axis=0, tiled=True)
    seq_count, length, width = everyone.shape
    total_rows = seq_count * length
    per_device = proj_weights.shape[2]
    accumulate = project_rows(everyone.reshape(total_rows, width))
    start_sum = jnp.zeros((3, total_rows, per_device), jnp.float32)
    projected = accumulate(
        start_sum, lax.all_gather(proj_weights, "seq", axis=1, tiled=True), jnp.int32(0)
    )
    queries = activate(projected[0], seq_count, length)
    keys_b = activate(projected[1], seq_count, length)
    values_b = to_heads(projected[2].astype(jnp.bfloat16), seq_count, length)
    prefix = block_prefix(keys_b, values_b)
    normed = attend(queries, keys_b, values_b, prefix, norm_gain)
    return lax.all_to_all(normed, "dp", split_axis=0, concat_axis=2, tiled=True)


def solution(mesh):
    in_specs = (P("dp", "seq", None), P(None, "seq", ("heads", "dp")), P(("heads", "dp")))
    out_specs = P("dp", "seq", "heads")
    return jax.shard_map(body, mesh=mesh, in_specs=in_specs, out_specs=out_specs, check_vma=False)
```

profile of v0, /device:TPU:0, one launch (start us, length us, event | category | flops | bytes accessed | tf_op | source)
XLA Modules:
  0.0 132.9 jit_solution(1204227285959018190)
XLA Ops:
  6.5 0.0 all-gather.5.cloned.1.call-start
  6.5 4.3 %copy.14 = bf16[3,1536,256]{1,2,0:T(8,128)(2,1)} copy(bf16[3,1536,256]{2,1,0:T(8,128)(2,1)} %param.6) | data formatting | bytes 4718592 | tf_op args[1]
  10.8 0.0 all-gather.5.cloned.1.call-update
  10.8 0.0 all-gather.7.cloned.1.call-start
  10.9 0.7 all-gather.7.cloned.1.call-update
  11.6 0.0 all-gather.9.cloned.1.call-start
  11.6 16.5 %all-gather.5.cloned.1.call-done = bf16[3,3072,256]{1,2,0:T(8,128)(2,1)} async-done(((bf16[3,1536,256]{1,2,0:T(8,128)(2,1)}), bf16[3,3072,256]{1,2,0:T(8,128)(2,1)}) %all-gather.5.cloned.1.call-update) | async-done | bytes 4718608 | tf_op jit(solution)/shard_map/all_gather | solution.py:70
  28.1 66.3 %all-gather.7.cloned.1.call-done = bf16[4,128,3072]{2,1,0:T(8,128)(2,1)} async-done(((bf16[1,128,3072]{2,1,0:T(8,128)(2,1)}), bf16[4,128,3072]{2,1,0:T(8,128)(2,1)}) %all-gather.7.cloned.1.call-update) | async-done | bytes 3145744 | tf_op jit(solution)/shard_map/all_gather | solution.py:63
  94.4 5.5 %convolution_bitcast_fusion = f32[3,512,256]{1,2,0:T(8,128)S(1)} fusion(bf16[3,3072,256]{1,2,0:T(8,128)(2,1)} %all-gather.5.cloned.1.call-done, bf16[512,3072,1]{1,0,2:T(8,128)(2,1)} %bitcast.33), kind=kOutput, calls=%fused_computation.1 | convolution fusion | flops 2415919104 | bytes 9437184 | tf_op jit(solution)/shard_map/nd,jdc->jnc/dot_general | solution.py:27
  99.9 0.1 fusion.8
  100.0 0.2 squeeze.12
  100.2 0.2 copy.18
  100.4 0.1 convert_element_type.22
  100.5 0.2 copy.21
  100.7 1.2 fusion.7
  101.9 0.0 all-gather.9.cloned.1.call-update
  101.9 0.2 squeeze.11
  102.1 0.2 copy.16
  102.4 0.6 fusion.2
  102.9 6.8 %all-gather.9.cloned.1.call-done = f32[8,2,128,128]{3,2,1,0:T(8,128)} async-done(((f32[4,2,128,128]{3,2,1,0:T(8,128)}), f32[8,2,128,128]{3,2,1,0:T(8,128)}) %all-gather.9.cloned.1.call-update) | async-done | bytes 1048592 | tf_op jit(solution)/shard_map/all_gather | solution.py:11
  109.8 0.0 copy-start
  109.8 0.4 multiply_reduce_fusion
  110.2 0.3 copy-done
  110.5 0.1 multiply_convert_fusion
  110.6 14.9 %all_to_all.18 = bf16[4,128,256]{1,2,0:T(8,128)(2,1)S(1)} all-to-all(bf16[4,128,256]{1,2,0:T(8,128)(2,1)S(1)} %bitcast.30), channel_id=1, replica_groups=mesh['seq'=2,'heads'=4,'dp'=4] {'dp'}, dimensions={0} | all-to-all | bytes 524288 | tf_op jit(solution)/shard_map/all_to_all | solution.py:77
  125.5 0.8 copy.26
  (5 shorter events, 0.1 us)
Async XLA Ops:
  6.5 21.6 %all-gather.5.cloned.1.call-start = ((), (), s32[]{:S(2)}) async-start(), calls=%async_computation.1 | async-start | bytes 7077888 | tf_op jit(solution)/shard_map/all_gather | solution.py:70
  10.8 83.6 %all-gather.7.cloned.1.call-start = ((), (), s32[]{:S(2)}) async-start(), calls=%async_computation.2 | async-start | bytes 3932160 | tf_op jit(solution)/shard_map/all_gather | solution.py:63
  11.6 98.2 %all-gather.9.cloned.1.call-start = ((), (), s32[]{:S(2)}) async-start(), calls=%async_computation.3 | async-start | bytes 1572864 | tf_op jit(solution)/shard_map/all_gather | solution.py:11
  109.8 0.7 copy-start
Sparse Core Ops, SparseCore 0:
  11.0 17.1 all-gather.4
  29.7 64.6 all-gather.6
  102.0 7.6 all-gather.8
where the time goes:
time: 133 us
  waiting for transfers between devices  90.3 us (68%)
  blocking collectives  14.9 us (11%)
  between operations  13.2 us (10%)
  matrix products  7.59 us (6%)
  local copies, waits for them, and re-layouts  6.62 us (5%)
    all_gather x1, waiting for transfers between devices, body(): everyone = lax.all_gather(tokens, 'dp', axis=0, tiled=True)  66.3 us
    all_gather x1, waiting for transfers between devices, body(): lax.all_gather(proj_weights, 'seq', axis=1, tiled=True)  16.5 us
    all_to_all x1, blocking collectives, body(): return lax.all_to_all(normed, 'dp', split_axis=0, concat_axis=2, tiled=True)  14.9 us
    all_gather x1, waiting for transfers between devices, prefix_2(): gathered = lax.all_gather(part, axis)  6.82 us
    dot_general x1, matrix products, accumulate(): jnp.einsum('nd,jdc->jnc', flat_rows, piece, preferred_element_type=jnp.fl...  5.47 us
    unnamed x3, local copies, waits for them, and re-layouts  4.56 us
  transfers between devices with their start and end apart: 3, of which 3 were waited for; matrix products, arithmetic and copies ran while one was open for 1% of the time, Pallas kernels for 0%

commit v1 on v0

v1 whole, which is shorter than its diff:
```python
import functools

import jax
import jax.numpy as jnp
from jax import lax
from jax.experimental import pallas as pl
from jax.experimental.pallas import tpu as pltpu
from jax.sharding import PartitionSpec as P

DH = 128
SUBS = 3
TURNS = SUBS + 1
MESH = pl.DeviceIdType.MESH


def kernel(
    sizes, tokens, weights, gain, out,
    tok, own, w, acc, queries, stage, state_out, state_in,
    own_sem, w_sem, w_send, w_recv, up_send, down_send, z_recv,
    x_send, x_recv, y_send, y_recv, st_send, st_recv, o_send, o_recv, o_sem,
):
    n_seq, n_heads, n_dp = sizes
    c, h, d = lax.axis_index("seq"), lax.axis_index("heads"), lax.axis_index("dp")
    length = own.shape[0]
    rows, cols = weights.shape[1], weights.shape[2]
    block = tok.shape[3]
    heads = cols // DH
    xp = h + 1 - 2 * (h % 2)
    yp = h + 2 - 4 * (h // 2)
    across = xp + yp - h

    def remote(src, dst, send, recv, **device):
        return pltpu.make_async_remote_copy(
            src_ref=src, dst_ref=dst, send_sem=send, recv_sem=recv,
            device_id=device, device_id_type=MESH,
        )

    own_copy = pltpu.make_async_copy(tokens.at[0], own, own_sem)
    own_copy.start()
    my_rows = w.at[:, pl.ds(pl.multiple_of(c * rows, 16), rows), :]
    w_copy = pltpu.make_async_copy(weights, my_rows, w_sem)
    w_copy.start()

    barrier = pltpu.get_barrier_semaphore()
    for o in range(1, n_dp):
        pl.semaphore_signal(barrier, inc=1, device_id={"dp": (d + o) % n_dp}, device_id_type=MESH)
    for o in range(1, n_seq):
        pl.semaphore_signal(barrier, inc=1, device_id={"seq": (c + o) % n_seq}, device_id_type=MESH)
    pl.semaphore_signal(barrier, inc=1, device_id={"heads": xp}, device_id_type=MESH)
    pl.semaphore_signal(barrier, inc=1, device_id={"heads": yp}, device_id_type=MESH)
    pl.semaphore_wait(barrier, n_dp + n_seq)

    def z_block(i):
        last = i // SUBS
        return (1 - last) * (h * SUBS + SUBS - 1 - i) + last * across * SUBS

    def x_block(i):
        last = i // SUBS
        return (1 - last) * (xp * SUBS + SUBS - 1 - i) + last * (across * SUBS + 1)

    def y_block(i):
        last = i // SUBS
        return (1 - last) * (yp * SUBS + SUBS - 1 - i) + last * (across * SUBS + 2)

    def first(i, up):
        b = z_block(i)
        src = tokens.at[0, :, pl.ds(pl.multiple_of(b * block, block), block)]
        return remote(
            src, tok.at[d, b], (up_send if up else down_send).at[d, i], z_recv.at[d, i],
            dp=d + 1 if up else d - 1,
        )

    def along(s, i, up):
        b = z_block(i)
        return remote(
            tok.at[s, b], tok.at[s, b], (up_send if up else down_send).at[s, i],
            z_recv.at[s, i], dp=d + 1 if up else d - 1,
        )

    def to_x(s, i, b):
        return remote(tok.at[s, b], tok.at[s, b], x_send.at[s, i], x_recv.at[s, i], heads=xp)

    def to_y(s, i, b):
        return remote(tok.at[s, b], tok.at[s, b], y_send.at[s, i], y_recv.at[s, i], heads=yp)

    for i in range(TURNS):
        @pl.when(d < n_dp - 1)
        def _():
            first(i, True).start()

        @pl.when(d > 0)
        def _():
            first(i, False).start()

    def share(o):
        return remote(
            weights, my_rows, w_send.at[o - 1], w_recv.at[o - 1], seq=(c + o) % n_seq
        )

    for o in range(1, n_seq):
        share(o).start()

    def for_sources(k, do):
        @pl.when(d - k >= 0)
        def _():
            do(d - k, True)

        @pl.when(d + k < n_dp)
        def _():
            do(d + k, False)

    def z_phase(t):
        i = t % TURNS

        def one(s, up):
            b = z_block(i)
            along(s, i, up).wait_recv()
            @pl.when(d < n_dp - 1 if up else d > 0)
            def _():
                along(s, i, up).start()

            @pl.when(i < SUBS)
            def _():
                to_x(s, i, b).start()
                to_y(s, i, b).start()

        for_sources(t // TURNS + 1, one)

    def xy_phase(t):
        i = t % TURNS

        def one(s, up):
            to_x(s, i, x_block(i)).wait_recv()

            @pl.when(i == 0)
            def _():
                to_y(s, SUBS, x_block(0)).start()

            to_y(s, i, y_block(i)).wait_recv()

            @pl.when(i == 1)
            def _():
                to_x(s, SUBS, y_block(1)).start()

        for_sources(t // TURNS + 1, one)

    def times(piece, b):
        k_rows = pl.ds(pl.multiple_of(b * block, block), block)
        return [
            jnp.dot(piece, w[j, k_rows, :], preferred_element_type=jnp.float32)
            for j in range(3)
        ]

    def add(s, i, parts):
        for j in range(3):
            new = parts[0][j] + parts[1][j] + parts[2][j]
            @pl.when(i == 0)
            def _():
                acc[s, j] = new

            @pl.when(i > 0)
            def _():
                acc[s, j] += new

    def state_to(s, o):
        return remote(
            state_out.at[s], state_in.at[o - 1, s], st_send.at[o - 1, s], st_recv.at[o - 1, s],
            seq=(c + o) % n_seq,
        )

    def silu(v):
        return v / (1.0 + jnp.exp(-v))

    def finish_local(s):
        causal = lax.broadcasted_iota(jnp.int32, (length, length), 0) >= lax.broadcasted_iota(
            jnp.int32, (length, length), 1
        )
        kept = []
        for head in range(heads):
            at = slice(head * DH, (head + 1) * DH)
            k = silu(acc[s, 1, :, at]).astype(jnp.bfloat16)
            v = acc[s, 2, :, at].astype(jnp.bfloat16)
            state = lax.dot_general(k, v, (((0,), (0,)), ((), ())), preferred_element_type=jnp.float32)
            state_out[s, head] = state.astype(jnp.bfloat16)
            kept.append((k, v))

        @pl.loop(1, n_seq - c)
        def _(o):
            state_to(s, o).start()

        for head in range(heads):
            at = slice(head * DH, (head + 1) * DH)
            k, v = kept[head]
            q = silu(acc[s, 0, :, at]).astype(jnp.bfloat16)
            scores = lax.dot_general(q, k, (((1,), (1,)), ((), ())), preferred_element_type=jnp.float32)
            scores_b = jnp.where(causal, scores, 0.0).astype(jnp.bfloat16)
            queries[s, :, at] = q
            acc[s, 0, :, at] = jnp.dot(scores_b, v, preferred_element_type=jnp.float32)

    def to_owner(s):
        at = pl.ds(pl.multiple_of(d * cols, cols), cols)
        return remote(stage.at[s], out.at[0, :, at], o_send.at[s], o_recv.at[d], dp=s)

    def keep(s):
        at = pl.ds(pl.multiple_of(d * cols, cols), cols)
        return pltpu.make_async_copy(stage.at[s], out.at[0, :, at], o_sem)

    def finish_carried(s):
        @pl.when(c > 0)
        def _():
            @pl.loop(1, c + 1)
            def _(o):
                state_to(s, o).wait_recv()

            for head in range(heads):
                at = slice(head * DH, (head + 1) * DH)
                prefix = lax.fori_loop(
                    1, c + 1,
                    lambda o, total: total + state_in[o - 1, s, head].astype(jnp.float32),
                    jnp.zeros((DH, DH), jnp.float32),
                )
                acc[s, 0, :, at] += jnp.dot(
                    queries[s, :, at], prefix.astype(jnp.bfloat16),
                    preferred_element_type=jnp.float32,
                )

        for head in range(heads):
            at = slice(head * DH, (head + 1) * DH)
            attn = acc[s, 0, :, at]
            scale = lax.rsqrt(jnp.mean(attn * attn, axis=-1, keepdims=True) + 1e-06)
            stage[s, :, at] = (attn * scale * gain[:, at]).astype(jnp.bfloat16)

    def compute(t):
        i = t % TURNS

        @pl.when(t < TURNS)
        def _():
            parts = []
            for n in range(SUBS):
                b = t * SUBS + n
                piece = own[:, pl.ds(pl.multiple_of(b * block, block), block)]
                parts.append(times(piece, b))
            add(d, i, parts)

            @pl.when(i == TURNS - 1)
            def _():
                finish_local(d)

        def one(s, up):
            blocks = (z_block(i), x_block(i), y_block(i))
            add(s, i, [times(tok[s, b], b) for b in blocks])

            @pl.when(i == TURNS - 1)
            def _():
                finish_local(s)

        for_sources(t // TURNS + 1, one)

    def output(t):
        @pl.when(t % TURNS == TURNS - 1)
        def _():
            @pl.when(t < TURNS)
            def _():
                finish_carried(d)
                keep(d).start()

            def one(s, up):
                finish_carried(s)
                to_owner(s).start()

            for_sources(t // TURNS + 1, one)

    turns = (n_dp - 1) * TURNS
    z_phase(0)
    z_phase(1)
    xy_phase(0)
    own_copy.wait()
    w_copy.wait()
    for o in range(1, n_seq):
        share(o).wait_recv()
    compute(0)

    @pl.loop(2, turns + 2)
    def _(t):
        @pl.when(t < turns)
        def _():
            z_phase(t)

        @pl.when(t <= turns)
        def _():
            xy_phase(t - 1)
            compute(t - 1)

        output(t - 2)

    for o in range(1, n_seq):
        share(o).wait_send()

    for i in range(TURNS):
        @pl.when(d < n_dp - 1)
        def _():
            first(i, True).wait_send()

        @pl.when(d > 0)
        def _():
            first(i, False).wait_send()

    @pl.loop(0, turns)
    def _(t):
        i = t % TURNS

        def one(s, up):
            @pl.when(d < n_dp - 1 if up else d > 0)
            def _():
                along(s, i, up).wait_send()

            to_x(s, i, z_block(i)).wait_send()
            to_y(s, i, z_block(i)).wait_send()

        for_sources(t // TURNS + 1, one)

    @pl.loop(0, n_dp)
    def _(s):
        @pl.loop(1, n_seq - c)
        def _(o):
            state_to(s, o).wait_send()

        @pl.when(s != d)
        def _():
            to_owner(s).wait_send()
            at = pl.ds(pl.multiple_of(s * cols, cols), cols)
            remote(stage.at[s], out.at[0, :, at], o_send.at[s], o_recv.at[s], dp=s).wait_recv()

    keep(d).wait()


def body(sizes, tokens, proj_weights, norm_gain):
    n_seq, n_heads, n_dp = sizes
    _, length, width = tokens.shape
    _, rows, cols = proj_weights.shape
    pieces = n_heads * SUBS
    block = width // pieces
    heads = cols // DH
    dma = pltpu.SemaphoreType.DMA
    any_space = pl.BlockSpec(memory_space=pl.ANY)
    flops = 2 * n_dp * length * width * 3 * cols
    return pl.pallas_call(
        functools.partial(kernel, sizes),
        out_shape=jax.ShapeDtypeStruct((1, length, n_dp * cols), jnp.bfloat16),
        in_specs=[any_space, any_space, pl.BlockSpec(memory_space=pltpu.VMEM)],
        out_specs=any_space,
        scratch_shapes=[
            pltpu.VMEM((n_dp, pieces, length, block), jnp.bfloat16),
            pltpu.VMEM((length, width), jnp.bfloat16),
            pltpu.VMEM((3, width, cols), jnp.bfloat16),
            pltpu.VMEM((n_dp, 3, length, cols), jnp.float32),
            pltpu.VMEM((n_dp, length, cols), jnp.bfloat16),
            pltpu.VMEM((n_dp, length, cols), jnp.bfloat16),
            pltpu.VMEM((n_dp, heads, DH, DH), jnp.bfloat16),
            pltpu.VMEM((n_seq - 1, n_dp, heads, DH, DH), jnp.bfloat16),
            dma, dma, dma((n_seq - 1,)), dma((n_seq - 1,)),
            dma((n_dp, TURNS)), dma((n_dp, TURNS)), dma((n_dp, TURNS)),
            dma((n_dp, TURNS)), dma((n_dp, TURNS)), dma((n_dp, TURNS)), dma((n_dp, TURNS)),
            dma((n_seq - 1, n_dp)), dma((n_seq - 1, n_dp)),
            dma((n_dp,)), dma((n_dp,)), dma,
        ],
        compiler_params=pltpu.CompilerParams(
            collective_id=0, has_side_effects=True, vmem_limit_bytes=48 * 1024 * 1024
        ),
        cost_estimate=pl.CostEstimate(
            flops=flops, bytes_accessed=2 * (tokens.size + proj_weights.size), transcendentals=0
        ),
    )(tokens, proj_weights, norm_gain.reshape(1, cols))


def solution(mesh):
    sizes = tuple(mesh.shape[name] for name in ("seq", "heads", "dp"))
    in_specs = (P("dp", "seq", None), P(None, "seq", ("heads", "dp")), P(("heads", "dp")))
    out_specs = P("dp", "seq", "heads")
    return jax.shard_map(
        functools.partial(body, sizes), mesh=mesh, in_specs=in_specs, out_specs=out_specs, check_vma=False
    )
```

time: 133 us -> 49.5 us (0.37)
  waiting for transfers between devices: 90.3 us -> 0 us
  Pallas kernels: 0 us -> 45.1 us
  blocking collectives: 14.9 us -> 0 us
  between operations: 13.2 us -> 0.01 us
  matrix products: 7.59 us -> 0 us
  local copies, waits for them, and re-layouts: 6.62 us -> 4.18 us
    all_gather x3 -> x0, waiting for transfers between devices: 89.6 us -> none  [the longest x1 66.3 us: body(): everyone = lax.all_gather(tokens, 'dp', axis=0, tiled=True)]
    pallas_call x0 -> x1, Pallas kernels: none -> 45.1 us  [body(): pl.pallas_call(functools.partial(kernel, sizes), out_shape=jax.ShapeDtype...]
    all_to_all x1 -> x0, blocking collectives: 14.9 us -> none  [body(): return lax.all_to_all(normed, 'dp', split_axis=0, concat_axis=2, tiled=True)]
    dot_general x4 -> x0, matrix products: 7.59 us -> none  [the longest x1 5.47 us: accumulate(): jnp.einsum('nd,jdc->jnc', flat_rows, piece, preferred_element_type=jnp.fl...]
    unnamed x3 -> x7, local copies, waits for them, and re-layouts: 4.56 us -> 4.18 us
  transfers between devices with their start and end apart: 3 -> 0, of which waited for: 3 -> 0; matrix products, arithmetic and copies ran while one was open for 1% -> 0% of each run, Pallas kernels for 0% -> 0%
where the time goes in v1:
time: 49.5 us; the launch traced here: 49.3 us
  Pallas kernels  45.1 us (91%)
  local copies, waits for them, and re-layouts  4.18 us (8%)
    pallas_call x1, Pallas kernels, body(): pl.pallas_call(functools.partial(kernel, sizes), out_shape=jax.ShapeDtype...  45.1 us
    unnamed x7, local copies, waits for them, and re-layouts  4.18 us

profile of v1, /device:TPU:0, one launch (start us, length us, event | category | flops | bytes accessed | tf_op | source)
XLA Modules:
  0.0 49.3 jit_solution(8508090874866587162)
XLA Ops:
  0.0 0.0 copy-start
  0.0 1.7 %copy-done = bf16[3,1536,256]{2,1,0:T(8,128)(2,1)S(1)} copy-done((bf16[3,1536,256]{2,1,0:T(8,128)(2,1)S(1)}, bf16[3,1536,256]{2,1,0:T(8,128)(2,1)}, u32[]{:S(2)}) %copy-start) | copy-done | bytes 2359320
  1.7 0.0 copy-start.1
  1.7 1.1 %copy-done.1 = bf16[1,128,3072]{2,1,0:T(8,128)(2,1)S(1)} copy-done((bf16[1,128,3072]{2,1,0:T(8,128)(2,1)S(1)}, bf16[1,128,3072]{2,1,0:T(8,128)(2,1)}, u32[]{:S(2)}) %copy-start.1) | copy-done | bytes 786456
  2.8 0.0 copy-start.2
  2.8 0.7 %copy-done.2 = f32[256]{0:T(256)S(1)} copy-done((f32[256]{0:T(256)S(1)}, f32[256]{0:T(256)}, u32[]{:S(2)}) %copy-start.2) | copy-done | bytes 1048
  3.5 45.1 %shard_map.37 = bf16[1,128,1024]{2,1,0:T(8,128)(2,1)S(1)} custom-call(bf16[1,128,3072]{2,1,0:T(8,128)(2,1)S(1)} %copy-done.1, bf16[3,1536,256]{2,1,0:T(8,128)(2,1)S(1)} %copy-done, f32[1,256]{1,0:T(1,128)S(1)} %bitcast.1), custom_call_target="tpu_custom_call" | custom-call | flops 2415919104 | bytes 3145728 | tf_op jit(solution)/shard_map/pallas_call | solution.py:347
  48.6 0.7 %copy.5 = bf16[1,128,1024]{2,1,0:T(8,128)(2,1)} copy(bf16[1,128,1024]{2,1,0:T(8,128)(2,1)S(1)} %shard_map.37) | data formatting | bytes 524288
Async XLA Ops:
  0.0 1.7 %copy-start = (bf16[3,1536,256]{2,1,0:T(8,128)(2,1)S(1)}, bf16[3,1536,256]{2,1,0:T(8,128)(2,1)}, u32[]{:S(2)}) copy-start(bf16[3,1536,256]{2,1,0:T(8,128)(2,1)} %weights.1) | copy-start | bytes 7077892
  1.7 1.1 %copy-start.1 = (bf16[1,128,3072]{2,1,0:T(8,128)(2,1)S(1)}, bf16[1,128,3072]{2,1,0:T(8,128)(2,1)}, u32[]{:S(2)}) copy-start(bf16[1,128,3072]{2,1,0:T(8,128)(2,1)} %tokens.1) | copy-start | bytes 2359300
  2.8 0.7 %copy-start.2 = (f32[256]{0:T(256)S(1)}, f32[256]{0:T(256)}, u32[]{:S(2)}) copy-start(f32[256]{0:T(256)} %param.5) | copy-start | bytes 3076

commit v2 on v1

--- a/solution.py
+++ b/solution.py
@@ -10,6 +10,10 @@
 DH = 128
 SUBS = 3
 TURNS = SUBS + 1
+LAG = 2
+START = 5
+EVEN = 2 * START - LAG
+OWN_AT = 1
 MESH = pl.DeviceIdType.MESH
 
 
@@ -92,13 +96,17 @@
         def _():
             first(i, False).start()
 
-    def share(o):
+    def share(o, j):
         return remote(
-            weights, my_rows, w_send.at[o - 1], w_recv.at[o - 1], seq=(c + o) % n_seq
+            weights.at[j], my_rows.at[j], w_send.at[o - 1, j], w_recv.at[o - 1, j],
+            seq=(c + o) % n_seq,
         )
 
     for o in range(1, n_seq):
-        share(o).start()
+        for j in range(3):
+            share(o, j).start()
+
+    acc[...] = jnp.zeros_like(acc)
 
     def for_sources(k, do):
         @pl.when(d - k >= 0)
@@ -151,16 +159,9 @@
             for j in range(3)
         ]
 
-    def add(s, i, parts):
+    def add(s, parts):
         for j in range(3):
-            new = parts[0][j] + parts[1][j] + parts[2][j]
-            @pl.when(i == 0)
-            def _():
-                acc[s, j] = new
-
-            @pl.when(i > 0)
-            def _():
-                acc[s, j] += new
+            acc[s, j] += parts[0][j] + parts[1][j] + parts[2][j]
 
     def state_to(s, o):
         return remote(
@@ -233,14 +234,14 @@
     def compute(t):
         i = t % TURNS
 
-        @pl.when(t < TURNS)
+        @pl.when(t // TURNS == OWN_AT)
         def _():
             parts = []
             for n in range(SUBS):
-                b = t * SUBS + n
+                b = i * SUBS + n
                 piece = own[:, pl.ds(pl.multiple_of(b * block, block), block)]
                 parts.append(times(piece, b))
-            add(d, i, parts)
+            add(d, parts)
 
             @pl.when(i == TURNS - 1)
             def _():
@@ -248,7 +249,7 @@
 
         def one(s, up):
             blocks = (z_block(i), x_block(i), y_block(i))
-            add(s, i, [times(tok[s, b], b) for b in blocks])
+            add(s, [times(tok[s, b], b) for b in blocks])
 
             @pl.when(i == TURNS - 1)
             def _():
@@ -259,7 +260,7 @@
     def output(t):
         @pl.when(t % TURNS == TURNS - 1)
         def _():
-            @pl.when(t < TURNS)
+            @pl.when(t // TURNS == OWN_AT)
             def _():
                 finish_carried(d)
                 keep(d).start()
@@ -271,30 +272,44 @@
             for_sources(t // TURNS + 1, one)
 
     turns = (n_dp - 1) * TURNS
-    z_phase(0)
-    z_phase(1)
-    xy_phase(0)
+    for t in range(START):
+        z_phase(t)
+        if t >= LAG:
+            xy_phase(t - LAG)
     own_copy.wait()
     w_copy.wait()
     for o in range(1, n_seq):
-        share(o).wait_recv()
-    compute(0)
-
-    @pl.loop(2, turns + 2)
+        for j in range(3):
+            share(o, j).wait_recv()
+
+    @pl.loop(START, EVEN)
+    def _(t):
+        z_phase(t)
+        xy_phase(t - LAG)
+
+        @pl.loop(0, 2)
+        def _(n):
+            @pl.when(t > START)
+            def _():
+                output(2 * (t - 1 - START) + n)
+
+            compute(2 * (t - START) + n)
+
+    @pl.loop(EVEN, turns + LAG)
     def _(t):
         @pl.when(t < turns)
         def _():
             z_phase(t)
 
-        @pl.when(t <= turns)
-        def _():
-            xy_phase(t - 1)
-            compute(t - 1)
-
-        output(t - 2)
+        xy_phase(t - LAG)
+        output(t - LAG - 1)
+        compute(t - LAG)
+
+    output(turns - 1)
 
     for o in range(1, n_seq):
-        share(o).wait_send()
+        for j in range(3):
+            share(o, j).wait_send()
 
     for i in range(TURNS):
         @pl.when(d < n_dp - 1)
@@ -342,13 +357,13 @@
     block = width // pieces
     heads = cols // DH
     dma = pltpu.SemaphoreType.DMA
-    any_space = pl.BlockSpec(memory_space=pl.ANY)
+    hbm = pl.BlockSpec(memory_space=pltpu.HBM)
     flops = 2 * n_dp * length * width * 3 * cols
     return pl.pallas_call(
         functools.partial(kernel, sizes),
         out_shape=jax.ShapeDtypeStruct((1, length, n_dp * cols), jnp.bfloat16),
-        in_specs=[any_space, any_space, pl.BlockSpec(memory_space=pltpu.VMEM)],
-        out_specs=any_space,
+        in_specs=[hbm, hbm, pl.BlockSpec(memory_space=pltpu.VMEM)],
+        out_specs=hbm,
         scratch_shapes=[
             pltpu.VMEM((n_dp, pieces, length, block), jnp.bfloat16),
             pltpu.VMEM((length, width), jnp.bfloat16),
@@ -358,14 +373,14 @@
             pltpu.VMEM((n_dp, length, cols), jnp.bfloat16),
             pltpu.VMEM((n_dp, heads, DH, DH), jnp.bfloat16),
             pltpu.VMEM((n_seq - 1, n_dp, heads, DH, DH), jnp.bfloat16),
-            dma, dma, dma((n_seq - 1,)), dma((n_seq - 1,)),
+            dma, dma, dma((n_seq - 1, 3)), dma((n_seq - 1, 3)),
             dma((n_dp, TURNS)), dma((n_dp, TURNS)), dma((n_dp, TURNS)),
             dma((n_dp, TURNS)), dma((n_dp, TURNS)), dma((n_dp, TURNS)), dma((n_dp, TURNS)),
             dma((n_seq - 1, n_dp)), dma((n_seq - 1, n_dp)),
             dma((n_dp,)), dma((n_dp,)), dma,
         ],
         compiler_params=pltpu.CompilerParams(
-            collective_id=0, has_side_effects=True, vmem_limit_bytes=48 * 1024 * 1024
+            collective_id=0, has_side_effects=True, vmem_limit_bytes=64 * 1024 * 1024
         ),
         cost_estimate=pl.CostEstimate(
             flops=flops, bytes_accessed=2 * (tokens.size + proj_weights.size), transcendentals=0

time: 49.5 us -> 44.1 us (0.89)
  Pallas kernels: 45.1 us -> 42.3 us
  local copies, waits for them, and re-layouts: 4.18 us -> 1.67 us
    pallas_call x1, Pallas kernels: 45.1 us -> 42.3 us  [body(): pl.pallas_call(functools.partial(kernel, sizes), out_shape=jax.ShapeDtype...]
    unnamed x7 -> x1, local copies, waits for them, and re-layouts: 4.18 us -> 1.67 us
where the time goes in v2:
time: 44.1 us; the launch traced here: 44 us
  Pallas kernels  42.3 us (96%)
  local copies, waits for them, and re-layouts  1.67 us (4%)
    pallas_call x1, Pallas kernels, body(): pl.pallas_call(functools.partial(kernel, sizes), out_shape=jax.ShapeDtype...  42.3 us
    unnamed x1, local copies, waits for them, and re-layouts  1.67 us

profile of v2, /device:TPU:0, one launch (start us, length us, event | category | flops | bytes accessed | tf_op | source)
XLA Modules:
  0.0 44.0 jit_solution(13131691102856850402)
XLA Ops:
  0.0 42.3 %shard_map.37 = bf16[1,128,1024]{2,1,0:T(8,128)(2,1)} custom-call(bf16[1,128,3072]{2,1,0:T(8,128)(2,1)} %tokens.1, bf16[3,1536,256]{2,1,0:T(8,128)(2,1)} %weights.1, f32[1,256]{1,0:T(1,128)} %bitcast.1), custom_call_target="tpu_custom_call" | custom-call | flops 2415919104 | bytes 3145728 | tf_op jit(solution)/shard_map/pallas_call | solution.py:362
  42.3 1.7 %copy.5 = bf16[1,128,1024]{2,1,0:T(8,128)(2,1)} copy(bf16[1,128,1024]{2,1,0:T(8,128)(2,1)} %shard_map.37) | data formatting | bytes 524288

commit v3 on v2

--- a/solution.py
+++ b/solution.py
@@ -13,13 +13,13 @@
 LAG = 2
 START = 5
 EVEN = 2 * START - LAG
-OWN_AT = 1
+OWN_AT = 2
 MESH = pl.DeviceIdType.MESH
 
 
 def kernel(
     sizes, tokens, weights, gain, out,
-    tok, own, w, acc, queries, stage, state_out, state_in,
+    tok, own, w, acc, queries, keys, values, stage, state_out, state_in,
     own_sem, w_sem, w_send, w_recv, up_send, down_send, z_recv,
     x_send, x_recv, y_send, y_recv, st_send, st_recv, o_send, o_recv, o_sem,
 ):
@@ -152,16 +152,38 @@
 
         for_sources(t // TURNS + 1, one)
 
-    def times(piece, b):
-        k_rows = pl.ds(pl.multiple_of(b * block, block), block)
-        return [
-            jnp.dot(piece, w[j, k_rows, :], preferred_element_type=jnp.float32)
-            for j in range(3)
-        ]
-
-    def add(s, parts):
-        for j in range(3):
-            acc[s, j] += parts[0][j] + parts[1][j] + parts[2][j]
+    def rows_of(s, blocks):
+        return jnp.concatenate([tok[s, b] for b in blocks], axis=1)
+
+    def own_rows(blocks):
+        return jnp.concatenate(
+            [own[:, pl.ds(pl.multiple_of(b * block, block), block)] for b in blocks], axis=1
+        )
+
+    def multiply(i, blocks, parts):
+        piece = jnp.concatenate([rows for _, rows in parts], axis=0)
+
+        def add(j):
+            k_rows = [pl.ds(pl.multiple_of(b * block, block), block) for b in blocks]
+            weight = jnp.concatenate([w[j, at, :] for at in k_rows], axis=0)
+            product = jnp.dot(piece, weight, preferred_element_type=jnp.float32)
+            for n, (s, _) in enumerate(parts):
+                acc[s, j] += product[n * length:(n + 1) * length]
+
+        add(1)
+        add(2)
+
+        @pl.when(i == TURNS - 1)
+        def _():
+            for s, _ in parts:
+                make_state(s)
+
+        add(0)
+
+        @pl.when(i == TURNS - 1)
+        def _():
+            for s, _ in parts:
+                finish_local(s)
 
     def state_to(s, o):
         return remote(
@@ -172,31 +194,35 @@
     def silu(v):
         return v / (1.0 + jnp.exp(-v))
 
-    def finish_local(s):
-        causal = lax.broadcasted_iota(jnp.int32, (length, length), 0) >= lax.broadcasted_iota(
-            jnp.int32, (length, length), 1
-        )
-        kept = []
+    def make_state(s):
         for head in range(heads):
             at = slice(head * DH, (head + 1) * DH)
             k = silu(acc[s, 1, :, at]).astype(jnp.bfloat16)
             v = acc[s, 2, :, at].astype(jnp.bfloat16)
             state = lax.dot_general(k, v, (((0,), (0,)), ((), ())), preferred_element_type=jnp.float32)
             state_out[s, head] = state.astype(jnp.bfloat16)
-            kept.append((k, v))
+            keys[s, :, at] = k
+            values[s, :, at] = v
 
         @pl.loop(1, n_seq - c)
         def _(o):
             state_to(s, o).start()
 
+    def finish_local(s):
+        causal = lax.broadcasted_iota(jnp.int32, (length, length), 0) >= lax.broadcasted_iota(
+            jnp.int32, (length, length), 1
+        )
         for head in range(heads):
             at = slice(head * DH, (head + 1) * DH)
-            k, v = kept[head]
             q = silu(acc[s, 0, :, at]).astype(jnp.bfloat16)
-            scores = lax.dot_general(q, k, (((1,), (1,)), ((), ())), preferred_element_type=jnp.float32)
+            scores = lax.dot_general(
+                q, keys[s, :, at], (((1,), (1,)), ((), ())), preferred_element_type=jnp.float32
+            )
             scores_b = jnp.where(causal, scores, 0.0).astype(jnp.bfloat16)
             queries[s, :, at] = q
-            acc[s, 0, :, at] = jnp.dot(scores_b, v, preferred_element_type=jnp.float32)
+            acc[s, 0, :, at] = jnp.dot(
+                scores_b, values[s, :, at], preferred_element_type=jnp.float32
+            )
 
     def to_owner(s):
         at = pl.ds(pl.multiple_of(d * cols, cols), cols)
@@ -233,34 +259,36 @@
 
     def compute(t):
         i = t % TURNS
-
-        @pl.when(t // TURNS == OWN_AT)
-        def _():
-            parts = []
-            for n in range(SUBS):
-                b = i * SUBS + n
-                piece = own[:, pl.ds(pl.multiple_of(b * block, block), block)]
-                parts.append(times(piece, b))
-            add(d, parts)
-
-            @pl.when(i == TURNS - 1)
-            def _():
-                finish_local(d)
-
-        def one(s, up):
-            blocks = (z_block(i), x_block(i), y_block(i))
-            add(s, [times(tok[s, b], b) for b in blocks])
-
-            @pl.when(i == TURNS - 1)
-            def _():
-                finish_local(s)
-
-        for_sources(t // TURNS + 1, one)
+        k = t // TURNS + 1
+        blocks = (z_block(i), x_block(i), y_block(i))
+        below = (d + n_dp - k) // n_dp
+        above = (2 * n_dp - 1 - d - k) // n_dp
+
+        @pl.when(below + above == 2)
+        def _():
+            multiply(i, blocks, [(s, rows_of(s, blocks)) for s in (d - k, d + k)])
+
+        @pl.when(below + above == 1)
+        def _():
+            s = d + k - 2 * k * below
+
+            @pl.when(k == OWN_AT)
+            def _():
+                multiply(i, blocks, [(d, own_rows(blocks)), (s, rows_of(s, blocks))])
+
+            @pl.when(k != OWN_AT)
+            def _():
+                multiply(i, blocks, [(s, rows_of(s, blocks))])
+
+        if 2 * OWN_AT < n_dp:
+            @pl.when((k == OWN_AT) & (below + above != 1))
+            def _():
+                multiply(i, blocks, [(d, own_rows(blocks))])
 
     def output(t):
         @pl.when(t % TURNS == TURNS - 1)
         def _():
-            @pl.when(t // TURNS == OWN_AT)
+            @pl.when(t // TURNS + 1 == OWN_AT)
             def _():
                 finish_carried(d)
                 keep(d).start()
@@ -295,15 +323,27 @@
 
             compute(2 * (t - START) + n)
 
-    @pl.loop(EVEN, turns + LAG)
+    late = turns - TURNS
+
+    @pl.loop(EVEN, late + 1)
     def _(t):
-        @pl.when(t < turns)
-        def _():
-            z_phase(t)
-
+        z_phase(t)
         xy_phase(t - LAG)
         output(t - LAG - 1)
         compute(t - LAG)
+
+    xy_phase(late - 1)
+    compute(late - 1)
+
+    @pl.loop(late + 1, turns + 1)
+    def _(t):
+        @pl.when(t < turns)
+        def _():
+            z_phase(t)
+
+        xy_phase(t - 1)
+        output(t - 2)
+        compute(t - 1)
 
     output(turns - 1)
 
@@ -371,6 +411,8 @@
             pltpu.VMEM((n_dp, 3, length, cols), jnp.float32),
             pltpu.VMEM((n_dp, length, cols), jnp.bfloat16),
             pltpu.VMEM((n_dp, length, cols), jnp.bfloat16),
+            pltpu.VMEM((n_dp, length, cols), jnp.bfloat16),
+            pltpu.VMEM((n_dp, length, cols), jnp.bfloat16),
             pltpu.VMEM((n_dp, heads, DH, DH), jnp.bfloat16),
             pltpu.VMEM((n_seq - 1, n_dp, heads, DH, DH), jnp.bfloat16),
             dma, dma, dma((n_seq - 1, 3)), dma((n_seq - 1, 3)),
@@ -380,7 +422,7 @@
             dma((n_dp,)), dma((n_dp,)), dma,
         ],
         compiler_params=pltpu.CompilerParams(
-            collective_id=0, has_side_effects=True, vmem_limit_bytes=64 * 1024 * 1024
+            collective_id=0, has_side_effects=True, vmem_limit_bytes=(64 * 1024 - 512) * 1024
         ),
         cost_estimate=pl.CostEstimate(
             flops=flops, bytes_accessed=2 * (tokens.size + proj_weights.size), transcendentals=0

time: 44.1 us -> 42.9 us (0.973)
  Pallas kernels: 42.3 us -> 41.1 us
    pallas_call x1, Pallas kernels: 42.3 us -> 41.1 us  [body(): pl.pallas_call(functools.partial(kernel, sizes), out_shape=jax.ShapeDtype...]
where the time goes in v3:
time: 42.9 us; the launch traced here: 42.8 us
  Pallas kernels  41.1 us (96%)
  local copies, waits for them, and re-layouts  1.67 us (4%)
    pallas_call x1, Pallas kernels, body(): pl.pallas_call(functools.partial(kernel, sizes), out_shape=jax.ShapeDtype...  41.1 us
    unnamed x1, local copies, waits for them, and re-layouts  1.67 us

profile of v3, /device:TPU:0, one launch (start us, length us, event | category | flops | bytes accessed | tf_op | source)
XLA Modules:
  0.0 42.8 jit_solution(17943840099152598572)
XLA Ops:
  0.0 41.1 %shard_map.37 = bf16[1,128,1024]{2,1,0:T(8,128)(2,1)} custom-call(bf16[1,128,3072]{2,1,0:T(8,128)(2,1)} %tokens.1, bf16[3,1536,256]{2,1,0:T(8,128)(2,1)} %weights.1, f32[1,256]{1,0:T(1,128)} %bitcast.1), custom_call_target="tpu_custom_call" | custom-call | flops 2415919104 | bytes 3145728 | tf_op jit(solution)/shard_map/pallas_call | solution.py:402
  41.1 1.7 %copy.5 = bf16[1,128,1024]{2,1,0:T(8,128)(2,1)} copy(bf16[1,128,1024]{2,1,0:T(8,128)(2,1)} %shard_map.37) | data formatting | bytes 524288

commit v4 on v3

--- a/solution.py
+++ b/solution.py
@@ -11,8 +11,6 @@
 SUBS = 3
 TURNS = SUBS + 1
 LAG = 2
-START = 5
-EVEN = 2 * START - LAG
 OWN_AT = 2
 MESH = pl.DeviceIdType.MESH
 
@@ -96,15 +94,20 @@
         def _():
             first(i, False).start()
 
-    def share(o, j):
+    part = min(rows, block)
+    parts = rows // part
+
+    def share(o, n):
+        at = pl.ds(pl.multiple_of(n // 3 * part, 16), part)
         return remote(
-            weights.at[j], my_rows.at[j], w_send.at[o - 1, j], w_recv.at[o - 1, j],
+            weights.at[n % 3, at], my_rows.at[n % 3, at], w_send.at[o - 1, n], w_recv.at[o - 1, n],
             seq=(c + o) % n_seq,
         )
 
     for o in range(1, n_seq):
-        for j in range(3):
-            share(o, j).start()
+        @pl.loop(0, 3 * parts)
+        def _(n):
+            share(o, n).start()
 
     acc[...] = jnp.zeros_like(acc)
 
@@ -160,14 +163,14 @@
             [own[:, pl.ds(pl.multiple_of(b * block, block), block)] for b in blocks], axis=1
         )
 
-    def multiply(i, blocks, parts):
-        piece = jnp.concatenate([rows for _, rows in parts], axis=0)
+    def multiply(i, blocks, group):
+        piece = jnp.concatenate([rows for _, rows in group], axis=0)
 
         def add(j):
             k_rows = [pl.ds(pl.multiple_of(b * block, block), block) for b in blocks]
             weight = jnp.concatenate([w[j, at, :] for at in k_rows], axis=0)
             product = jnp.dot(piece, weight, preferred_element_type=jnp.float32)
-            for n, (s, _) in enumerate(parts):
+            for n, (s, _) in enumerate(group):
                 acc[s, j] += product[n * length:(n + 1) * length]
 
         add(1)
@@ -175,14 +178,14 @@
 
         @pl.when(i == TURNS - 1)
         def _():
-            for s, _ in parts:
+            for s, _ in group:
                 make_state(s)
 
         add(0)
 
         @pl.when(i == TURNS - 1)
         def _():
-            for s, _ in parts:
+            for s, _ in group:
                 finish_local(s)
 
     def state_to(s, o):
@@ -300,56 +303,52 @@
             for_sources(t // TURNS + 1, one)
 
     turns = (n_dp - 1) * TURNS
-    for t in range(START):
+    late = turns - TURNS
+
+    @pl.loop(0, late + 1)
+    def _(t):
         z_phase(t)
-        if t >= LAG:
+
+        @pl.when(t >= LAG)
+        def _():
             xy_phase(t - LAG)
+
+    xy_phase(late - 1)
     own_copy.wait()
     w_copy.wait()
     for o in range(1, n_seq):
-        for j in range(3):
-            share(o, j).wait_recv()
-
-    @pl.loop(START, EVEN)
-    def _(t):
-        z_phase(t)
-        xy_phase(t - LAG)
-
-        @pl.loop(0, 2)
+        @pl.loop(0, 3 * parts)
         def _(n):
-            @pl.when(t > START)
-            def _():
-                output(2 * (t - 1 - START) + n)
-
-            compute(2 * (t - START) + n)
-
-    late = turns - TURNS
-
-    @pl.loop(EVEN, late + 1)
-    def _(t):
-        z_phase(t)
-        xy_phase(t - LAG)
-        output(t - LAG - 1)
-        compute(t - LAG)
-
-    xy_phase(late - 1)
-    compute(late - 1)
-
-    @pl.loop(late + 1, turns + 1)
-    def _(t):
+            share(o, n).wait_recv()
+
+    step = turns // TURNS
+
+    @pl.loop(0, TURNS)
+    def _(n):
+        t = late + 1 + n
+
         @pl.when(t < turns)
         def _():
             z_phase(t)
 
         xy_phase(t - 1)
-        output(t - 2)
-        compute(t - 1)
+
+        @pl.loop(0, step)
+        def _(m):
+            @pl.when(n > 0)
+            def _():
+                output((n - 1) * step + m)
+
+        @pl.loop(0, step)
+        def _(m):
+            compute(n * step + m)
 
     output(turns - 1)
 
     for o in range(1, n_seq):
-        for j in range(3):
-            share(o, j).wait_send()
+        @pl.loop(0, 3 * parts)
+        def _(n):
+            share(o, n).wait_send()
 
     for i in range(TURNS):
         @pl.when(d < n_dp - 1)
@@ -396,6 +395,7 @@
     pieces = n_heads * SUBS
     block = width // pieces
     heads = cols // DH
+    copies = 3 * (rows // min(rows, block))
     dma = pltpu.SemaphoreType.DMA
     hbm = pl.BlockSpec(memory_space=pltpu.HBM)
     flops = 2 * n_dp * length * width * 3 * cols
@@ -415,7 +415,7 @@
             pltpu.VMEM((n_dp, length, cols), jnp.bfloat16),
             pltpu.VMEM((n_dp, heads, DH, DH), jnp.bfloat16),
             pltpu.VMEM((n_seq - 1, n_dp, heads, DH, DH), jnp.bfloat16),
-            dma, dma, dma((n_seq - 1, 3)), dma((n_seq - 1, 3)),
+            dma, dma, dma((n_seq - 1, copies)), dma((n_seq - 1, copies)),
             dma((n_dp, TURNS)), dma((n_dp, TURNS)), dma((n_dp, TURNS)),
             dma((n_dp, TURNS)), dma((n_dp, TURNS)), dma((n_dp, TURNS)), dma((n_dp, TURNS)),
             dma((n_seq - 1, n_dp)), dma((n_seq - 1, n_dp)),

time: 42.9 us -> 46.9 us (1.093)
  Pallas kernels: 41.1 us -> 45.1 us
    pallas_call x1, Pallas kernels: 41.1 us -> 45.1 us  [body(): pl.pallas_call(functools.partial(kernel, sizes), out_shape=jax.ShapeDtype...]
where the time goes in v4:
time: 46.9 us; the launch traced here: 46.8 us
  Pallas kernels  45.1 us (96%)
  local copies, waits for them, and re-layouts  1.67 us (4%)
    pallas_call x1, Pallas kernels, body(): pl.pallas_call(functools.partial(kernel, sizes), out_shape=jax.ShapeDtype...  45.1 us
    unnamed x1, local copies, waits for them, and re-layouts  1.67 us

profile of v4, /device:TPU:0, one launch (start us, length us, event | category | flops | bytes accessed | tf_op | source)
XLA Modules:
  0.0 46.8 jit_solution(17323868369250864303)
XLA Ops:
  0.0 45.1 %shard_map.37 = bf16[1,128,1024]{2,1,0:T(8,128)(2,1)} custom-call(bf16[1,128,3072]{2,1,0:T(8,128)(2,1)} %tokens.1, bf16[3,1536,256]{2,1,0:T(8,128)(2,1)} %weights.1, f32[1,256]{1,0:T(1,128)} %bitcast.1), custom_call_target="tpu_custom_call" | custom-call | flops 2415919104 | bytes 3145728 | tf_op jit(solution)/shard_map/pallas_call | solution.py:402
  45.1 1.7 %copy.5 = bf16[1,128,1024]{2,1,0:T(8,128)(2,1)} copy(bf16[1,128,1024]{2,1,0:T(8,128)(2,1)} %shard_map.37) | data formatting | bytes 524288

commit v5 on v4

--- a/solution.py
+++ b/solution.py
@@ -11,7 +11,6 @@
 SUBS = 3
 TURNS = SUBS + 1
 LAG = 2
-OWN_AT = 2
 MESH = pl.DeviceIdType.MESH
 
 
@@ -275,27 +274,15 @@
         def _():
             s = d + k - 2 * k * below
 
-            @pl.when(k == OWN_AT)
-            def _():
-                multiply(i, blocks, [(d, own_rows(blocks)), (s, rows_of(s, blocks))])
-
-            @pl.when(k != OWN_AT)
-            def _():
-                multiply(i, blocks, [(s, rows_of(s, blocks))])
-
-        if 2 * OWN_AT < n_dp:
-            @pl.when((k == OWN_AT) & (below + above != 1))
-            def _():
-                multiply(i, blocks, [(d, own_rows(blocks))])
+            multiply(i, blocks, [(s, rows_of(s, blocks))])
+
+    def compute_own(i):
+        blocks = [i * SUBS + n for n in range(SUBS)]
+        multiply(i, blocks, [(d, own_rows(blocks))])
 
     def output(t):
         @pl.when(t % TURNS == TURNS - 1)
         def _():
-            @pl.when(t // TURNS + 1 == OWN_AT)
-            def _():
-                finish_carried(d)
-                keep(d).start()
-
             def one(s, up):
                 finish_carried(s)
                 to_owner(s).start()
@@ -305,15 +292,10 @@
     turns = (n_dp - 1) * TURNS
     late = turns - TURNS
 
-    @pl.loop(0, late + 1)
+    @pl.loop(0, late - TURNS)
     def _(t):
         z_phase(t)
 
-        @pl.when(t >= LAG)
-        def _():
-            xy_phase(t - LAG)
-
-    xy_phase(late - 1)
     own_copy.wait()
     w_copy.wait()
     for o in range(1, n_seq):
@@ -321,27 +303,37 @@
         def _(n):
             share(o, n).wait_recv()
 
-    step = turns // TURNS
-
-    @pl.loop(0, TURNS)
-    def _(n):
-        t = late + 1 + n
+    @pl.loop(late - TURNS, late)
+    def _(t):
+        z_phase(t)
+        compute_own(t - late + TURNS)
+
+        @pl.when(t >= late - LAG)
+        def _():
+            xy_phase(t - late + LAG)
+            compute(t - late + LAG)
+
+    @pl.loop(late, late + (turns - LAG) // 2)
+    def _(t):
+        done = LAG + 2 * (t - late)
 
         @pl.when(t < turns)
         def _():
             z_phase(t)
 
-        xy_phase(t - 1)
-
-        @pl.loop(0, step)
-        def _(m):
-            @pl.when(n > 0)
-            def _():
-                output((n - 1) * step + m)
-
-        @pl.loop(0, step)
-        def _(m):
-            compute(n * step + m)
+        @pl.when(t == late)
+        def _():
+            finish_carried(d)
+            keep(d).start()
+
+        @pl.loop(0, 2)
+        def _(n):
+            @pl.when(t > late)
+            def _():
+                output(done - 2 + n)
+
+            xy_phase(done + n)
+            compute(done + n)
 
     output(turns - 1)
 

time: 46.9 us -> 44.8 us (0.955)
  Pallas kernels: 45.1 us -> 43 us
    pallas_call x1, Pallas kernels: 45.1 us -> 43 us  [body(): pl.pallas_call(functools.partial(kernel, sizes), out_shape=jax.ShapeDtype...]
where the time goes in v5:
time: 44.8 us; the launch traced here: 44.7 us
  Pallas kernels  43 us (96%)
  local copies, waits for them, and re-layouts  1.67 us (4%)
    pallas_call x1, Pallas kernels, body(): pl.pallas_call(functools.partial(kernel, sizes), out_shape=jax.ShapeDtype...  43 us
    unnamed x1, local copies, waits for them, and re-layouts  1.67 us

profile of v5, /device:TPU:0, one launch (start us, length us, event | category | flops | bytes accessed | tf_op | source)
XLA Modules:
  0.0 44.7 jit_solution(10344105839341199455)
XLA Ops:
  0.0 43.0 %shard_map.37 = bf16[1,128,1024]{2,1,0:T(8,128)(2,1)} custom-call(bf16[1,128,3072]{2,1,0:T(8,128)(2,1)} %tokens.1, bf16[3,1536,256]{2,1,0:T(8,128)(2,1)} %weights.1, f32[1,256]{1,0:T(1,128)} %bitcast.1), custom_call_target="tpu_custom_call" | custom-call | flops 2415919104 | bytes 3145728 | tf_op jit(solution)/shard_map/pallas_call | solution.py:394
  43.0 1.7 %copy.5 = bf16[1,128,1024]{2,1,0:T(8,128)(2,1)} copy(bf16[1,128,1024]{2,1,0:T(8,128)(2,1)} %shard_map.37) | data formatting | bytes 524288

commit v6 on v3

--- a/solution.py
+++ b/solution.py
@@ -98,15 +98,15 @@
 
     def share(o, j):
         return remote(
-            weights.at[j], my_rows.at[j], w_send.at[o - 1, j], w_recv.at[o - 1, j],
+            my_rows.at[j], my_rows.at[j], w_send.at[o - 1, j], w_recv.at[o - 1, j],
             seq=(c + o) % n_seq,
         )
 
+    acc[...] = jnp.zeros_like(acc)
+    w_copy.wait()
     for o in range(1, n_seq):
         for j in range(3):
             share(o, j).start()
-
-    acc[...] = jnp.zeros_like(acc)
 
     def for_sources(k, do):
         @pl.when(d - k >= 0)
@@ -305,7 +305,6 @@
         if t >= LAG:
             xy_phase(t - LAG)
     own_copy.wait()
-    w_copy.wait()
     for o in range(1, n_seq):
         for j in range(3):
             share(o, j).wait_recv()
@@ -422,7 +421,7 @@
             dma((n_dp,)), dma((n_dp,)), dma,
         ],
         compiler_params=pltpu.CompilerParams(
-            collective_id=0, has_side_effects=True, vmem_limit_bytes=(64 * 1024 - 512) * 1024
+            collective_id=0, has_side_effects=True, vmem_limit_bytes=(64 * 1024 - 11008) * 1024
         ),
         cost_estimate=pl.CostEstimate(
             flops=flops, bytes_accessed=2 * (tokens.size + proj_weights.size), transcendentals=0

time: 42.9 us -> 41.9 us (0.977)
  Pallas kernels: 41.1 us -> 40.3 us
    pallas_call x1, Pallas kernels: 41.1 us -> 40.3 us  [body(): pl.pallas_call(functools.partial(kernel, sizes), out_shape=jax.ShapeDtype...]
    unnamed x1 -> x3, local copies, waits for them, and re-layouts: 1.67 us -> 1.38 us
where the time goes in v6:
time: 41.9 us; the launch traced here: 41.7 us
  Pallas kernels  40.3 us (96%)
  local copies, waits for them, and re-layouts  1.38 us (3%)
    pallas_call x1, Pallas kernels, body(): pl.pallas_call(functools.partial(kernel, sizes), out_shape=jax.ShapeDtype...  40.3 us
    unnamed x3, local copies, waits for them, and re-layouts  1.38 us

profile of v6, /device:TPU:0, one launch (start us, length us, event | category | flops | bytes accessed | tf_op | source)
XLA Modules:
  0.0 41.7 jit_solution(2897684142742731858)
XLA Ops:
  0.0 0.0 copy-start
  0.0 0.7 %copy-done = f32[256]{0:T(256)S(1)} copy-done((f32[256]{0:T(256)S(1)}, f32[256]{0:T(256)}, u32[]{:S(2)}) %copy-start) | copy-done | bytes 1048
  0.7 40.3 %shard_map.37 = bf16[1,128,1024]{2,1,0:T(8,128)(2,1)S(1)} custom-call(bf16[1,128,3072]{2,1,0:T(8,128)(2,1)} %tokens.1, bf16[3,1536,256]{2,1,0:T(8,128)(2,1)} %weights.1, f32[1,256]{1,0:T(1,128)S(1)} %bitcast.1), custom_call_target="tpu_custom_call" | custom-call | flops 2415919104 | bytes 3145728 | tf_op jit(solution)/shard_map/pallas_call | solution.py:401
  41.0 0.7 %copy.5 = bf16[1,128,1024]{2,1,0:T(8,128)(2,1)} copy(bf16[1,128,1024]{2,1,0:T(8,128)(2,1)S(1)} %shard_map.37) | data formatting | bytes 524288
Async XLA Ops:
  0.0 0.7 %copy-start = (f32[256]{0:T(256)S(1)}, f32[256]{0:T(256)}, u32[]{:S(2)}) copy-start(f32[256]{0:T(256)} %param.5) | copy-start | bytes 3076

commit v7 on v6

--- a/solution.py
+++ b/solution.py
@@ -11,7 +11,7 @@
 SUBS = 3
 TURNS = SUBS + 1
 LAG = 2
-START = 5
+START = 4
 EVEN = 2 * START - LAG
 OWN_AT = 2
 MESH = pl.DeviceIdType.MESH

time: 41.9 us -> 42.3 us (level)
  no operation moved by 1% of the time
where the time goes in v7:
time: 42.3 us; the launch traced here: 42.1 us
  Pallas kernels  40.7 us (96%)
  local copies, waits for them, and re-layouts  1.38 us (3%)
    pallas_call x1, Pallas kernels, body(): pl.pallas_call(functools.partial(kernel, sizes), out_shape=jax.ShapeDtype...  40.7 us
    unnamed x3, local copies, waits for them, and re-layouts  1.38 us

profile of v7, /device:TPU:0, one launch (start us, length us, event | category | flops | bytes accessed | tf_op | source)
XLA Modules:
  0.0 42.1 jit_solution(18285602507966629365)
XLA Ops:
  0.0 0.0 copy-start
  0.0 0.7 %copy-done = f32[256]{0:T(256)S(1)} copy-done((f32[256]{0:T(256)S(1)}, f32[256]{0:T(256)}, u32[]{:S(2)}) %copy-start) | copy-done | bytes 1048
  0.7 40.7 %shard_map.37 = bf16[1,128,1024]{2,1,0:T(8,128)(2,1)S(1)} custom-call(bf16[1,128,3072]{2,1,0:T(8,128)(2,1)} %tokens.1, bf16[3,1536,256]{2,1,0:T(8,128)(2,1)} %weights.1, f32[1,256]{1,0:T(1,128)S(1)} %bitcast.1), custom_call_target="tpu_custom_call" | custom-call | flops 2415919104 | bytes 3145728 | tf_op jit(solution)/shard_map/pallas_call | solution.py:401
  41.4 0.7 %copy.5 = bf16[1,128,1024]{2,1,0:T(8,128)(2,1)} copy(bf16[1,128,1024]{2,1,0:T(8,128)(2,1)S(1)} %shard_map.37) | data formatting | bytes 524288
Async XLA Ops:
  0.0 0.7 %copy-start = (f32[256]{0:T(256)S(1)}, f32[256]{0:T(256)}, u32[]{:S(2)}) copy-start(f32[256]{0:T(256)} %param.5) | copy-start | bytes 3076
